TPU v7x, 32 devices: a whole 2x2x4 slice. The times are simulated.
32 devices in a mesh: rep: 2 (over x), seq: 16 (over z, y, core).
Axes of the slice: x: 2, y: 2, z: 4, core: 2. Of those that a mesh axis runs over, the one named last changes fastest.
Arguments:
- keys: bfloat16 [2048, 5120], P(('rep', 'seq')), parts along dimension 0, may hold values from -36 to 36
- values: bfloat16 [2048, 5120], P(('rep', 'seq')), parts along dimension 0, may hold values from -6 to 6
- queries: bfloat16 [2, 1024, 5120], P(None, ('rep', 'seq')), parts along dimension 1, may hold values from -6 to 6
Outputs:
- attended: bfloat16 [2, 1024, 5120], P(None, ('rep', 'seq')), parts along dimension 1
There are 2 independent parts, one for each index of `rep`. A program takes and returns all parts, laid end to end along the dimension named above; each array names one. Nothing has to cross between parts.
All inputs are finite; a program needn't handle non-finite values.
Results may differ from a plain program's by a relative error of at most 0.0038.
Values may be sent and summed in bfloat16 or wider, within the bound.
No kernel may reach another device: no remote copies, remote signals or barrier semaphores. Data moves between devices by JAX's collectives and lax.ppermute only.
A program may use at most 128 MiB of HBM per device.

v0:
```python
import math

import jax
import jax.numpy as jnp
from jax import lax
from jax.sharding import PartitionSpec as P

HEAD_DIM = 128
GROUPS = 8


def local(keys, values, queries):
    nseq = lax.axis_size("seq")
    blocks = nseq // GROUPS
    ctx_rows, width = keys.shape
    group_width = width // GROUPS
    heads_group = group_width // HEAD_DIM
    layers, tok_rows, _ = queries.shape
    query_total = tok_rows * nseq
    scale = 1.0 / math.sqrt(HEAD_DIM)

    def arrange(local_block):
        return local_block.reshape(ctx_rows // blocks, nseq, group_width)

    def by_source(array):
        return array.reshape((array.shape[0], blocks, GROUPS) + array.shape[2:])

    moved_keys, moved_values = (
        lax.all_to_all(arrange(keys), "seq", split_axis=1, concat_axis=1, tiled=True),
        lax.all_to_all(arrange(values), "seq", split_axis=1, concat_axis=1, tiled=True),
    )
    moved_keys = moved_keys.reshape(-1, group_width)
    moved_values = moved_values.reshape(-1, group_width)
    layer_outs = []
    for layer in range(layers):
        local_query = queries[layer]
        per_group = local_query.reshape(tok_rows, GROUPS, group_width)
        received = lax.all_to_all(
            jnp.broadcast_to(per_group[:, None], (tok_rows, blocks, GROUPS, group_width)).reshape(
                tok_rows, nseq, group_width
            ),
            "seq",
            split_axis=1,
            concat_axis=0,
            tiled=True,
        )
        own_block = received.reshape(query_total, group_width)

        def one_head(head):
            start = head * HEAD_DIM
            q_head = lax.dynamic_slice_in_dim(own_block, start, HEAD_DIM, 1)
            k_head = lax.dynamic_slice_in_dim(moved_keys, start, HEAD_DIM, 1)
            v_head = lax.dynamic_slice_in_dim(moved_values, start, HEAD_DIM, 1)
            scores = (
                lax.dot_general(
                    q_head, k_head, (((1,), (1,)), ((), ())), preferred_element_type=jnp.float32
                )
                * scale
            )
            peak = jnp.max(scores, axis=1)
            expo = jnp.exp(scores - peak[:, None])
            total = jnp.sum(expo, axis=1)
            summed = jnp.dot(expo.astype(jnp.bfloat16), v_head, preferred_element_type=jnp.float32)
            return (summed, peak, total)

        summed, peak, total = lax.map(one_head, jnp.arange(heads_group, dtype=jnp.int32))
        shaped = (
            summed.reshape(heads_group, nseq, tok_rows, HEAD_DIM),
            peak.reshape(heads_group, nseq, tok_rows),
            total.reshape(heads_group, nseq, tok_rows),
        )
        combine_summed = lax.all_to_all(shaped[0], "seq", split_axis=1, concat_axis=1, tiled=True)
        combine_peak = lax.all_to_all(shaped[1], "seq", split_axis=1, concat_axis=1, tiled=True)
        combine_total = lax.all_to_all(shaped[2], "seq", split_axis=1, concat_axis=1, tiled=True)
        rows = combine_peak.shape[2]
        summed_s = by_source(combine_summed)
        peak_s = by_source(combine_peak)
        total_s = by_source(combine_total)
        highest = jnp.max(peak_s, axis=1)
        factor = jnp.exp(peak_s - highest[:, None])
        denom = jnp.sum(factor * total_s, axis=1)
        numer = jnp.sum(factor[..., None] * summed_s, axis=1)
        result = numer / denom[..., None]
        result = jnp.transpose(result, (2, 1, 0, 3)).reshape(rows, GROUPS * heads_group * HEAD_DIM)
        mixed = result.astype(jnp.bfloat16)
        layer_outs.append(mixed)
    return jnp.stack(layer_outs)


def solution(mesh):
    return jax.shard_map(
        local,
        mesh=mesh,
        in_specs=(P(("rep", "seq"), None), P(("rep", "seq"), None), P(None, ("rep", "seq"), None)),
        out_specs=P(None, ("rep", "seq"), None),
        check_vma=False,
    )
```

profile of v0, /device:TPU:0, one launch (start us, length us, event | category | flops | bytes accessed | tf_op | source)
XLA Modules:
  0.0 212.6 jit_solution(11663222374262786308)
XLA Ops:
  0.0 1.4 reshape.112
  2.4 7.4 %all-to-all-start.1 = ((bf16[32,16,640]{2,0,1:T(8,128)(2,1)}), bf16[32,16,640]{2,0,1:T(8,128)(2,1)S(1)}, u32[]{:S(2)}, u32[]{:S(2)}) async-start(bf16[32,16,640]{2,0,1:T(8,128)(2,1)} %copy.39), calls=%async_computation.1 | async-start | bytes 1310720 | tf_op jit(solution)/shard_map/all_to_all | solution.py:29
  11.1 15.3 %all-to-all-done.1 = bf16[32,16,640]{2,0,1:T(8,128)(2,1)S(1)} async-done(((bf16[32,16,640]{2,0,1:T(8,128)(2,1)}), bf16[32,16,640]{2,0,1:T(8,128)(2,1)S(1)}, u32[]{:S(2)}, u32[]{:S(2)}) %all-to-all-start.1) | async-done | bytes 655392 | tf_op jit(solution)/shard_map/all_to_all | solution.py:29
  26.4 4.8 %all-to-all-start.2 = ((bf16[32,16,640]{2,0,1:T(8,128)(2,1)}), bf16[32,16,640]{2,0,1:T(8,128)(2,1)S(1)}, u32[]{:S(2)}, u32[]{:S(2)}) async-start(bf16[32,16,640]{2,0,1:T(8,128)(2,1)} %copy.41), calls=%async_computation.2 | async-start | bytes 1310720 | tf_op jit(solution)/shard_map/all_to_all | solution.py:30
  31.3 16.4 %all-to-all-done.2 = bf16[32,16,640]{2,0,1:T(8,128)(2,1)S(1)} async-done(((bf16[32,16,640]{2,0,1:T(8,128)(2,1)}), bf16[32,16,640]{2,0,1:T(8,128)(2,1)S(1)}, u32[]{:S(2)}, u32[]{:S(2)}) %all-to-all-start.2) | async-done | bytes 655392 | tf_op jit(solution)/shard_map/all_to_all | solution.py:30
  48.7 4.8 %all-to-all-start = ((bf16[32,16,640]{2,0,1:T(8,128)(2,1)}), bf16[32,16,640]{2,0,1:T(8,128)(2,1)S(1)}, u32[]{:S(2)}, u32[]{:S(2)}) async-start(bf16[32,16,640]{2,0,1:T(8,128)(2,1)} %bitcast.8), calls=%async_computation | async-start | bytes 1310720 | tf_op jit(solution)/shard_map/all_to_all | solution.py:38
  54.0 16.1 %all-to-all-done = bf16[32,16,640]{2,0,1:T(8,128)(2,1)S(1)} async-done(((bf16[32,16,640]{2,0,1:T(8,128)(2,1)}), bf16[32,16,640]{2,0,1:T(8,128)(2,1)S(1)}, u32[]{:S(2)}, u32[]{:S(2)}) %all-to-all-start) | async-done | bytes 655392 | tf_op jit(solution)/shard_map/all_to_all | solution.py:38
  71.0 4.8 %all-to-all-start.6 = ((bf16[32,16,640]{2,0,1:T(8,128)(2,1)}), bf16[32,16,640]{2,0,1:T(8,128)(2,1)S(1)}, u32[]{:S(2)}, u32[]{:S(2)}) async-start(bf16[32,16,640]{2,0,1:T(8,128)(2,1)} %bitcast.20), calls=%async_computation.6 | async-start | bytes 1310720 | tf_op jit(solution)/shard_map/all_to_all | solution.py:38
  75.9 15.8 %while.28 = (s32[]{:T(128)}, f32[5,512,128]{2,1,0:T(8,128)S(1)}, f32[5,512]{1,0:T(8,128)S(1)}, f32[5,512]{1,0:T(8,128)S(1)}, s32[5]{0:T(128)S(1)}, /*index=5*/bf...) while((s32[]{:T(128)}, f32[5,512,128]{2,1,0:T(8,128)S(1)}, ...), condition=%wide.region_3.4_spmd, body=%wide.region_0.3_spmd.sunk | while | flops 135789568 | bytes 3818687 | solution.py:66
  83.5 1.2 fusion.45
  86.6 1.2 fusion.45
  92.7 6.0 %all-to-all-start.3 = ((f32[16,1,160]{2,1,0:T(1,128)}), f32[16,1,160]{2,1,0:T(1,128)S(1)}, u32[]{:S(2)}, u32[]{:S(2)}) async-start(f32[16,1,160]{2,1,0:T(1,128)} %reshape.134), calls=%async_computation.3 | async-start | bytes 32768 | tf_op jit(solution)/shard_map/all_to_all | solution.py:73
  99.5 5.7 %all-to-all-done.3 = f32[16,1,160]{2,1,0:T(1,128)S(1)} async-done(((f32[16,1,160]{2,1,0:T(1,128)}), f32[16,1,160]{2,1,0:T(1,128)S(1)}, u32[]{:S(2)}, u32[]{:S(2)}) %all-to-all-start.3) | async-done | bytes 10272 | tf_op jit(solution)/shard_map/all_to_all | solution.py:73
  105.2 3.5 %all-to-all-start.5 = ((f32[16,1,160]{2,1,0:T(1,128)}), f32[16,1,160]{2,1,0:T(1,128)S(1)}, u32[]{:S(2)}, u32[]{:S(2)}) async-start(f32[16,1,160]{2,1,0:T(1,128)} %reshape.136), calls=%async_computation.5 | async-start | bytes 32768 | tf_op jit(solution)/shard_map/all_to_all | solution.py:74
  108.9 11.4 %while.29 = (s32[]{:T(128)}, f32[5,512,128]{2,1,0:T(8,128)S(1)}, f32[5,512]{1,0:T(8,128)S(1)}, f32[5,512]{1,0:T(8,128)S(1)}, s32[5]{0:T(128)S(1)}, /*index=5*/bf...) while((s32[]{:T(128)}, f32[5,512,128]{2,1,0:T(8,128)S(1)}, ...), condition=%wide.region_10.11_spmd, body=%wide.region_7.10_spmd.sunk | while | flops 135789568 | bytes 3818687 | solution.py:66
  121.3 6.0 %all-to-all-start.7 = ((f32[16,1,160]{2,1,0:T(1,128)}), f32[16,1,160]{2,1,0:T(1,128)S(1)}, u32[]{:S(2)}, u32[]{:S(2)}) async-start(f32[16,1,160]{2,1,0:T(1,128)} %reshape.130), calls=%async_computation.7 | async-start | bytes 32768 | tf_op jit(solution)/shard_map/all_to_all | solution.py:73
  128.1 5.7 %all-to-all-done.7 = f32[16,1,160]{2,1,0:T(1,128)S(1)} async-done(((f32[16,1,160]{2,1,0:T(1,128)}), f32[16,1,160]{2,1,0:T(1,128)S(1)}, u32[]{:S(2)}, u32[]{:S(2)}) %all-to-all-start.7) | async-done | bytes 10272 | tf_op jit(solution)/shard_map/all_to_all | solution.py:73
  133.8 3.5 %all-to-all-start.9 = ((f32[16,1,160]{2,1,0:T(1,128)}), f32[16,1,160]{2,1,0:T(1,128)S(1)}, u32[]{:S(2)}, u32[]{:S(2)}) async-start(f32[16,1,160]{2,1,0:T(1,128)} %reshape.132), calls=%async_computation.9 | async-start | bytes 32768 | tf_op jit(solution)/shard_map/all_to_all | solution.py:74
  137.3 2.5 %copy.46 = f32[5,16,32,128]{3,2,0,1:T(8,128)} copy(f32[5,16,32,128]{3,2,1,0:T(8,128)} %bitcast.89) | data formatting | bytes 2621440 | tf_op jit(solution)/shard_map/reshape | solution.py:68
  139.8 4.0 %all-to-all-done.9 = f32[16,1,160]{2,1,0:T(1,128)S(1)} async-done(((f32[16,1,160]{2,1,0:T(1,128)}), f32[16,1,160]{2,1,0:T(1,128)S(1)}, u32[]{:S(2)}, u32[]{:S(2)}) %all-to-all-start.9) | async-done | bytes 10272 | tf_op jit(solution)/shard_map/all_to_all | solution.py:74
  143.8 3.8 %all-to-all-start.4 = ((f32[5,16,32,128]{3,2,0,1:T(8,128)}), f32[5,16,32,128]{3,2,0,1:T(8,128)S(1)}, u32[]{:S(2)}, u32[]{:S(2)}) async-start(f32[5,16,32,128]{3,2,0,1:T(8,128)} %copy.46), calls=%async_computation.4 | async-start | bytes 2621440 | tf_op jit(solution)/shard_map/all_to_all | solution.py:72
  148.8 26.2 %all-to-all-done.4 = f32[5,16,32,128]{3,2,0,1:T(8,128)S(1)} async-done(((f32[5,16,32,128]{3,2,0,1:T(8,128)}), f32[5,16,32,128]{3,2,0,1:T(8,128)S(1)}, u32[]{:S(2)}, u32[]{:S(2)}) %all-to-all-start.4) | async-done | bytes 1310752 | tf_op jit(solution)/shard_map/all_to_all | solution.py:72
  175.0 8.0 %all-to-all-start.8 = ((f32[5,16,32,128]{3,2,0,1:T(8,128)}), f32[5,16,32,128]{3,2,0,1:T(8,128)S(1)}, u32[]{:S(2)}, u32[]{:S(2)}) async-start(f32[5,16,32,128]{3,2,0,1:T(8,128)} %copy.55), calls=%async_computation.8 | async-start | bytes 2621440 | tf_op jit(solution)/shard_map/all_to_all | solution.py:72
  188.0 22.4 %all-to-all-done.8 = f32[5,16,32,128]{3,2,0,1:T(8,128)S(1)} async-done(((f32[5,16,32,128]{3,2,0,1:T(8,128)}), f32[5,16,32,128]{3,2,0,1:T(8,128)S(1)}, u32[]{:S(2)}, u32[]{:S(2)}) %all-to-all-start.8) | async-done | bytes 1310752 | tf_op jit(solution)/shard_map/all_to_all | solution.py:72
  (129 shorter events, 34.7 us)
Async XLA Ops:
  1.4 8.4 %copy-start.4 = (bf16[64,5120]{1,0:T(8,128)(2,1)S(1)}, bf16[64,5120]{1,0:T(8,128)(2,1)}, u32[]{:S(2)}) copy-start(bf16[64,5120]{1,0:T(8,128)(2,1)} %param.8) | copy-start | bytes 1966084
  2.4 24.0 %all-to-all-start.1 = ((bf16[32,16,640]{2,0,1:T(8,128)(2,1)}), bf16[32,16,640]{2,0,1:T(8,128)(2,1)S(1)}, u32[]{:S(2)}, u32[]{:S(2)}) async-start(bf16[32,16,640]{2,0,1:T(8,128)(2,1)} %copy.39), calls=%async_computation.1 | async-start | bytes 1310720 | tf_op jit(solution)/shard_map/all_to_all | solution.py:29
  10.1 21.1 %copy-start.5 = (bf16[2,32,5120]{2,1,0:T(8,128)(2,1)S(1)}, bf16[2,32,5120]{2,1,0:T(8,128)(2,1)}, u32[]{:S(2)}) copy-start(bf16[2,32,5120]{2,1,0:T(8,128)(2,1)} %param.9) | copy-start | bytes 1966084
  26.4 21.4 %all-to-all-start.2 = ((bf16[32,16,640]{2,0,1:T(8,128)(2,1)}), bf16[32,16,640]{2,0,1:T(8,128)(2,1)S(1)}, u32[]{:S(2)}, u32[]{:S(2)}) async-start(bf16[32,16,640]{2,0,1:T(8,128)(2,1)} %copy.41), calls=%async_computation.2 | async-start | bytes 1310720 | tf_op jit(solution)/shard_map/all_to_all | solution.py:30
  48.7 21.4 %all-to-all-start = ((bf16[32,16,640]{2,0,1:T(8,128)(2,1)}), bf16[32,16,640]{2,0,1:T(8,128)(2,1)S(1)}, u32[]{:S(2)}, u32[]{:S(2)}) async-start(bf16[32,16,640]{2,0,1:T(8,128)(2,1)} %bitcast.8), calls=%async_computation | async-start | bytes 1310720 | tf_op jit(solution)/shard_map/all_to_all | solution.py:38
  70.0 5.7 %copy-start.3 = (bf16[32,16,640]{2,0,1:T(8,128)(2,1)}, bf16[32,16,640]{2,0,1:T(8,128)(2,1)S(1)}, u32[]{:S(2)}) copy-start(bf16[32,16,640]{2,0,1:T(8,128)(2,1)S(1)} %all-to-all-done) | copy-start | bytes 1966084
  71.0 21.7 %all-to-all-start.6 = ((bf16[32,16,640]{2,0,1:T(8,128)(2,1)}), bf16[32,16,640]{2,0,1:T(8,128)(2,1)S(1)}, u32[]{:S(2)}, u32[]{:S(2)}) async-start(bf16[32,16,640]{2,0,1:T(8,128)(2,1)} %bitcast.20), calls=%async_computation.6 | async-start | bytes 1310720 | tf_op jit(solution)/shard_map/all_to_all | solution.py:38
  91.7 17.0 %copy-start.2 = (f32[5,512,128]{2,1,0:T(8,128)}, f32[5,512,128]{2,1,0:T(8,128)S(1)}, u32[]{:S(2)}) copy-start(f32[5,512,128]{2,1,0:T(8,128)S(1)} %get-tuple-element.94) | copy-start | bytes 3932164
  92.7 12.5 %all-to-all-start.3 = ((f32[16,1,160]{2,1,0:T(1,128)}), f32[16,1,160]{2,1,0:T(1,128)S(1)}, u32[]{:S(2)}, u32[]{:S(2)}) async-start(f32[16,1,160]{2,1,0:T(1,128)} %reshape.134), calls=%async_computation.3 | async-start | bytes 32768 | tf_op jit(solution)/shard_map/all_to_all | solution.py:73
  105.2 16.1 %all-to-all-start.5 = ((f32[16,1,160]{2,1,0:T(1,128)}), f32[16,1,160]{2,1,0:T(1,128)S(1)}, u32[]{:S(2)}, u32[]{:S(2)}) async-start(f32[16,1,160]{2,1,0:T(1,128)} %reshape.136), calls=%async_computation.5 | async-start | bytes 32768 | tf_op jit(solution)/shard_map/all_to_all | solution.py:74
  120.3 19.5 %copy-start = (f32[5,512,128]{2,1,0:T(8,128)}, f32[5,512,128]{2,1,0:T(8,128)S(1)}, u32[]{:S(2)}) copy-start(f32[5,512,128]{2,1,0:T(8,128)S(1)} %get-tuple-element.97) | copy-start | bytes 3932164
  121.3 12.5 %all-to-all-start.7 = ((f32[16,1,160]{2,1,0:T(1,128)}), f32[16,1,160]{2,1,0:T(1,128)S(1)}, u32[]{:S(2)}, u32[]{:S(2)}) async-start(f32[16,1,160]{2,1,0:T(1,128)} %reshape.130), calls=%async_computation.7 | async-start | bytes 32768 | tf_op jit(solution)/shard_map/all_to_all | solution.py:73
  133.8 10.0 %all-to-all-start.9 = ((f32[16,1,160]{2,1,0:T(1,128)}), f32[16,1,160]{2,1,0:T(1,128)S(1)}, u32[]{:S(2)}, u32[]{:S(2)}) async-start(f32[16,1,160]{2,1,0:T(1,128)} %reshape.132), calls=%async_computation.9 | async-start | bytes 32768 | tf_op jit(solution)/shard_map/all_to_all | solution.py:74
  143.8 3.8 %copy-start.1 = (f32[5,512,128]{2,1,0:T(8,128)S(1)}, f32[5,512,128]{2,1,0:T(8,128)}, u32[]{:S(2)}) copy-start(f32[5,512,128]{2,1,0:T(8,128)} %copy-done) | copy-start | bytes 3932164
  143.8 31.2 %all-to-all-start.4 = ((f32[5,16,32,128]{3,2,0,1:T(8,128)}), f32[5,16,32,128]{3,2,0,1:T(8,128)S(1)}, u32[]{:S(2)}, u32[]{:S(2)}) async-start(f32[5,16,32,128]{3,2,0,1:T(8,128)} %copy.46), calls=%async_computation.4 | async-start | bytes 2621440 | tf_op jit(solution)/shard_map/all_to_all | solution.py:72
  175.0 35.4 %all-to-all-start.8 = ((f32[5,16,32,128]{3,2,0,1:T(8,128)}), f32[5,16,32,128]{3,2,0,1:T(8,128)S(1)}, u32[]{:S(2)}, u32[]{:S(2)}) async-start(f32[5,16,32,128]{3,2,0,1:T(8,128)} %copy.55), calls=%async_computation.8 | async-start | bytes 2621440 | tf_op jit(solution)/shard_map/all_to_all | solution.py:72
where the time goes:
time: 216 us; the launch traced here: 213 us
  waiting for transfers between devices  112 us (52%)
  starting transfers between devices  52.5 us (24%)
  local copies, waits for them, and re-layouts  22.8 us (11%)
  matrix products  11.3 us (5%)
  other arithmetic  6.99 us (3%)
  loops' own time  6.76 us (3%)
    all_to_all x2, waiting for transfers between devices, local(): lax.all_to_all(shaped[0], 'seq', split_axis=1, concat_axis=1, tiled=True)  48.6 us
    all_to_all x1, waiting for transfers between devices, local(): lax.all_to_all(arrange(values), 'seq', split_axis=1, concat_axis=1, tiled...  16.4 us
    all_to_all x2, waiting for transfers between devices, local(): lax.all_to_all(jnp.broadcast_to(per_group[:, None], (tok_rows, blocks, GR...  16.1 us
    all_to_all x1, waiting for transfers between devices, local(): lax.all_to_all(arrange(keys), 'seq', split_axis=1, concat_axis=1, tiled=T...  15.3 us
    all_to_all x2, starting transfers between devices, local(): lax.all_to_all(shaped[1], 'seq', split_axis=1, concat_axis=1, tiled=True)  12 us
    all_to_all x2, starting transfers between devices, local(): lax.all_to_all(shaped[0], 'seq', split_axis=1, concat_axis=1, tiled=True)  11.8 us
    all_to_all x2, waiting for transfers between devices, local(): lax.all_to_all(shaped[1], 'seq', split_axis=1, concat_axis=1, tiled=True)  11.4 us
    all_to_all x2, starting transfers between devices, local(): lax.all_to_all(jnp.broadcast_to(per_group[:, None], (tok_rows, blocks, GR...  9.54 us
  transfers between devices with their start and end apart: 10, of which 8 were waited for; matrix products, arithmetic and copies ran while one was open for 16% of the time, Pallas kernels for 0%

commit v1 on v0

v1 whole, which is shorter than its diff:
```python
import functools
import math

import jax
import jax.numpy as jnp
from jax import lax
from jax.experimental import pallas as pl
from jax.experimental.pallas import tpu as pltpu
from jax.sharding import Mesh, PartitionSpec as P

HEAD_DIM = 128
GROUPS = 8
SUB = 128
F32 = jnp.float32


def attend_head(partial, q_ref, ka_ref, va_ref, kb_ref, vb_ref, o_ref, *stat_refs):
    src, rows, _ = q_ref.shape
    q = q_ref[...].reshape(src * rows, HEAD_DIM)
    ka, va, kb, vb = (r[...].reshape(-1, HEAD_DIM) for r in (ka_ref, va_ref, kb_ref, vb_ref))
    factor = math.log2(math.e) / math.sqrt(HEAD_DIM)
    nt = (((1,), (1,)), ((), ()))
    outs = []
    for at in range(0, src * rows, SUB):
        part = q[at : at + SUB]
        sa = lax.dot_general(part, ka, nt, preferred_element_type=F32)
        sb = lax.dot_general(part, kb, nt, preferred_element_type=F32)
        peak = jnp.maximum(jnp.max(sa, axis=1, keepdims=True), jnp.max(sb, axis=1, keepdims=True))
        ea = jnp.exp2((sa - peak) * factor)
        eb = jnp.exp2((sb - peak) * factor)
        total = jnp.sum(ea, axis=1, keepdims=True) + jnp.sum(eb, axis=1, keepdims=True)
        acc = jnp.dot(ea.astype(jnp.bfloat16), va, preferred_element_type=F32)
        acc = acc + jnp.dot(eb.astype(jnp.bfloat16), vb, preferred_element_type=F32)
        if not partial:
            acc = acc / total
        outs.append(acc)
        if partial:
            stat_refs[0][at : at + SUB] = jnp.broadcast_to(peak * factor, (SUB, HEAD_DIM))
            stat_refs[1][at : at + SUB] = jnp.broadcast_to(total, (SUB, HEAD_DIM))
    o_ref[...] = jnp.concatenate(outs, axis=0).reshape(o_ref.shape).astype(o_ref.dtype)


def attend(got, other, rows_kv, rows_q, partial):
    chips, _, width = got.shape
    heads = width // HEAD_DIM
    own_kv = got[:, : 2 * rows_kv].reshape(chips, 2, rows_kv, width)
    own_q = got[:, 2 * rows_kv :]
    other = other.reshape(chips, 2, rows_kv, width)

    def kv(which):
        return pl.BlockSpec((chips, None, rows_kv, HEAD_DIM), lambda h: (0, which, 0, h))

    q_spec = pl.BlockSpec((chips, rows_q, HEAD_DIM), lambda h: (0, 0, h))
    dtype = F32 if partial else jnp.bfloat16
    out_shape = [jax.ShapeDtypeStruct((chips, rows_q, width), dtype)]
    out_specs = [pl.BlockSpec((chips, rows_q, HEAD_DIM), lambda h: (0, 0, h))]
    if partial:
        out_shape += [jax.ShapeDtypeStruct((heads, chips * rows_q, HEAD_DIM), F32)] * 2
        out_specs += [pl.BlockSpec((None, chips * rows_q, HEAD_DIM), lambda h: (h, 0, 0))] * 2
    queries, keys = chips * rows_q, 2 * chips * rows_kv
    return pl.pallas_call(
        functools.partial(attend_head, partial),
        grid=(heads,),
        in_specs=[q_spec, kv(0), kv(1), kv(0), kv(1)],
        out_specs=out_specs,
        out_shape=out_shape,
        compiler_params=pltpu.CompilerParams(vmem_limit_bytes=40 * 2**20),
        cost_estimate=pl.CostEstimate(
            flops=4 * queries * keys * width,
            bytes_accessed=2 * width * (2 * queries + 2 * keys),
            transcendentals=heads * queries * keys,
        ),
    )(own_q, own_kv, own_kv, other, other)


def local(keys, values, queries):
    chips = lax.axis_size("chip")
    blocks = chips // GROUPS
    ctx_rows, width = keys.shape
    gw = width // GROUPS
    heads = gw // HEAD_DIM
    layers, tok_rows, _ = queries.shape
    rows_q = layers * tok_rows
    rows_kv = ctx_rows // blocks
    partial = blocks > 1

    def by_chip(array):
        return jnp.swapaxes(array.reshape(rows_kv, chips, gw), 0, 1)

    q = jnp.swapaxes(queries.reshape(rows_q, GROUPS, gw), 0, 1)
    q = jnp.broadcast_to(q[None], (blocks, GROUPS, rows_q, gw)).reshape(chips, rows_q, gw)
    packed = jnp.concatenate([by_chip(keys), by_chip(values), q], axis=1)
    got = lax.all_to_all(packed, "chip", split_axis=0, concat_axis=0, tiled=True)
    other = lax.ppermute(got[:, : 2 * rows_kv], "core", [(0, 1), (1, 0)])
    outs = attend(got, other, rows_kv, rows_q, partial)
    if not partial:
        back = lax.all_to_all(outs[0], "chip", split_axis=0, concat_axis=0, tiled=True)
        return jnp.swapaxes(back, 0, 1).reshape(layers, tok_rows, width)
    stats = [jnp.moveaxis(s[:, :, 0].reshape(heads, chips, rows_q), 0, 2) for s in outs[1:]]
    stats = jnp.concatenate(stats, axis=2)
    stats = jnp.pad(stats, ((0, 0), (0, 0), (0, -2 * heads % HEAD_DIM)))
    sent = jnp.concatenate([outs[0], stats], axis=2)
    back = lax.all_to_all(sent, "chip", split_axis=0, concat_axis=0, tiled=True)
    back = back.reshape(blocks, GROUPS, rows_q, -1)
    summed = back[..., :gw].reshape(blocks, GROUPS, rows_q, heads, HEAD_DIM)
    peak = back[..., gw : gw + heads]
    total = back[..., gw + heads : gw + 2 * heads]
    share = jnp.exp2(peak - jnp.max(peak, axis=0))
    denom = jnp.sum(share * total, axis=0)
    numer = jnp.sum(share[..., None] * summed, axis=0)
    result = (numer / denom[..., None]).astype(jnp.bfloat16)
    return jnp.swapaxes(result.reshape(GROUPS, rows_q, gw), 0, 1).reshape(layers, tok_rows, width)


def solution(mesh):
    rep, seq = mesh.shape["rep"], mesh.shape["seq"]
    by_core = Mesh(mesh.devices.reshape(rep, seq // 2, 2), ("rep", "chip", "core"))
    rows = ("rep", "chip", "core")
    return jax.shard_map(
        local,
        mesh=by_core,
        in_specs=(P(rows, None), P(rows, None), P(None, rows, None)),
        out_specs=P(None, rows, None),
        check_vma=False,
    )
```

time: 216 us -> 89.1 us (0.41); the launches traced: 213 us -> 88.9 us
  waiting for transfers between devices: 112 us -> 2.95 us
  blocking collectives: 0 us -> 73.9 us
  starting transfers between devices: 52.5 us -> 0.07 us
  local copies, waits for them, and re-layouts: 22.8 us -> 3.31 us
  matrix products: 11.3 us -> 0 us
  Pallas kernels: 0 us -> 8.41 us
  other arithmetic: 6.99 us -> 0.17 us
  loops' own time: 6.76 us -> 0 us
    all_to_all x10 -> x0, waiting for transfers between devices: 112 us -> none  [the longest x2 48.6 us: local(): lax.all_to_all(shaped[0], 'seq', split_axis=1, concat_axis=1, tiled=True)]
    all_to_all x0 -> x2, blocking collectives: none -> 73.9 us  [the longest x1 52.9 us: local(): lax.all_to_all(packed, 'chip', split_axis=0, concat_axis=0, tiled=True)]
    all_to_all x10 -> x0, starting transfers between devices: 52.5 us -> none  [the longest x2 12 us: local(): lax.all_to_all(shaped[1], 'seq', split_axis=1, concat_axis=1, tiled=True)]
    dot_general x20 -> x0, matrix products: 11.3 us -> none  [the longest x10 7.66 us: one_head(): lax.dot_general(q_head, k_head, (((1,), (1,)), ((), ())), preferred_eleme...]
    pallas_call x0 -> x1, Pallas kernels: none -> 8.41 us  [attend(): pl.pallas_call(functools.partial(attend_head, partial), grid=(heads,), in...]
    another operation x2 -> x0, loops' own time: 6.76 us -> none  [local(): lax.map(one_head, jnp.arange(heads_group, dtype=jnp.int32))]
    reshape x14 -> x2, local copies, waits for them, and re-layouts: 7.66 us -> 1.21 us  [the longest x1 1.14 us: local(): return jnp.swapaxes(back, 0, 1).reshape(layers, tok_rows, width)]
    dynamic_slice x10 -> x0, local copies, waits for them, and re-layouts: 6.08 us -> none  [local(): lax.map(one_head, jnp.arange(heads_group, dtype=jnp.int32))]
  transfers between devices with their start and end apart: 10 -> 1, of which waited for: 8 -> 1; matrix products, arithmetic and copies ran while one was open for 16% -> 0% of each run, Pallas kernels for 0% -> 0%
where the time goes in v1:
time: 89.1 us; the launch traced here: 88.9 us
  blocking collectives  73.9 us (83%)
  Pallas kernels  8.41 us (9%)
  local copies, waits for them, and re-layouts  3.31 us (4%)
  waiting for transfers between devices  2.95 us (3%)
    all_to_all x1, blocking collectives, local(): lax.all_to_all(packed, 'chip', split_axis=0, concat_axis=0, tiled=True)  52.9 us
    all_to_all x1, blocking collectives, local(): lax.all_to_all(outs[0], 'chip', split_axis=0, concat_axis=0, tiled=True)  21 us
    pallas_call x1, Pallas kernels, attend(): pl.pallas_call(functools.partial(attend_head, partial), grid=(heads,), in...  8.41 us
    ppermute x1, waiting for transfers between devices, local(): other = lax.ppermute(got[:, :2 * rows_kv], 'core', [(0, 1), (1, 0)])  2.95 us
  transfers between devices with their start and end apart: 1, of which 1 were waited for; matrix products, arithmetic and copies ran while one was open for 0% of the time, Pallas kernels for 0%

profile of v1, /device:TPU:0, one launch (start us, length us, event | category | flops | bytes accessed | tf_op | source)
XLA Modules:
  0.0 88.9 jit_solution(3396148873464917705)
XLA Ops:
  0.0 0.0 copy-start
  0.0 0.0 copy-start.1
  0.0 1.3 %copy.10 = bf16[8,8,8,640]{3,2,1,0:T(8,128)(2,1)S(1)} copy(bf16[8,8,8,640]{3,1,2,0:T(8,128)(2,1)} %bitcast.28) | data formatting | bytes 1310720
  1.3 0.1 copy.14
  1.4 0.0 copy-done
  1.4 0.1 copy-done.1
  1.5 0.2 bitcast_bitcast_fusion
  1.7 0.2 pad_maximum_fusion
  1.8 52.9 %all_to_all.10 = bf16[8,192,640]{2,1,0:T(8,128)(2,1)S(1)} all-to-all(bf16[8,192,640]{2,1,0:T(8,128)(2,1)S(1)} %pad_maximum_fusion), channel_id=1, replica_groups=mesh['rep'=2,'chip'=8,'core'=2] {'chip'}, dimensions={0} | all-to-all | bytes 3932160 | tf_op jit(solution)/shard_map/all_to_all | solution.py:93
  54.7 0.1 slice.10
  54.8 0.1 collective-permute-start
  54.9 0.1 slice.9.q_ref
  55.0 3.0 %collective-permute-done = bf16[8,128,640]{2,1,0:T(8,128)(2,1)S(1)} collective-permute-done((bf16[8,128,640]{2,1,0:T(8,128)(2,1)S(1)}, bf16[8,128,640]{2,1,0:T(8,128)(2,1)S(1)}, u32[]{:S(2)}, u32[]{:S(2)}) %collective-permute-start) | collective-permute-done | bytes 1310752 | tf_op jit(solution)/shard_map/ppermute | solution.py:94
  57.9 8.4 %shard_map.37 = bf16[8,64,640]{2,1,0:T(8,128)(2,1)S(1)} custom-call(bf16[8,64,640]{2,1,0:T(8,128)(2,1)S(1)} %slice.9.q_ref, bf16[8,2,64,640]{3,2,1,0:T(8,128)(2,1)S(1)} %bitcast.19, bf16[8,2,64,640]{3,2,1,0:T(8,128)(2,1)S(1)} %bitcast.20, bf16[8,2,64,640]{3,2,1,0:T(8,128)(2,1)S(1)} %bitcast.21, bf16[8,2,64,640]{3,2,1,0:T(8,128)(2,1)S(1)} %bitcast.22), custom_call_target="tpu_custom_call" | custom-call | flops 1342177280 | bytes 3932160 | tf_op jit(solution)/shard_map/pallas_call | solution.py:61
  66.4 21.0 %all_to_all.11 = bf16[8,64,640]{2,1,0:T(8,128)(2,1)S(1)} all-to-all(bf16[8,64,640]{2,1,0:T(8,128)(2,1)S(1)} %shard_map.37), channel_id=1, replica_groups=mesh['rep'=2,'chip'=8,'core'=2] {'chip'}, dimensions={0} | all-to-all | bytes 1310720 | tf_op jit(solution)/shard_map/all_to_all | solution.py:97
  87.3 0.4 copy.7
  87.7 1.1 %reshape.23 = bf16[2,32,5120]{2,1,0:T(8,128)(2,1)} reshape(bf16[64,8,640]{2,1,0:T(8,128)(2,1)S(1)} %copy.7) | data formatting | bytes 1310720 | tf_op jit(solution)/shard_map/reshape | solution.py:98
Async XLA Ops:
  0.0 1.4 %copy-start = (bf16[64,5120]{1,0:T(8,128)(2,1)S(1)}, bf16[64,5120]{1,0:T(8,128)(2,1)}, u32[]{:S(2)}) copy-start(bf16[64,5120]{1,0:T(8,128)(2,1)} %param.4) | copy-start | bytes 1966084
  0.0 1.5 %copy-start.1 = (bf16[64,5120]{1,0:T(8,128)(2,1)S(1)}, bf16[64,5120]{1,0:T(8,128)(2,1)}, u32[]{:S(2)}) copy-start(bf16[64,5120]{1,0:T(8,128)(2,1)} %param.3) | copy-start | bytes 1966084
  54.8 3.1 %collective-permute-start = (bf16[8,128,640]{2,1,0:T(8,128)(2,1)S(1)}, bf16[8,128,640]{2,1,0:T(8,128)(2,1)S(1)}, u32[]{:S(2)}, u32[]{:S(2)}) collective-permute-start(bf16[8,128,640]{2,1,0:T(8,128)(2,1)S(1)} %slice.10), channel_id=1, source_target_pairs={{0,1},{1,0},{2,3},{3,2},{4,5},{5,4},{6,7},{7,6},{8,9},{9,8},{10,11... | collective-permute-start | bytes 3932168 | tf_op jit(solution)/shard_map/ppermute | solution.py:94

commit v2 on v1

v2 whole, which is shorter than its diff:
```python
import functools
import math

import jax
import jax.numpy as jnp
from jax import lax
from jax.experimental import pallas as pl
from jax.experimental.pallas import tpu as pltpu
from jax.sharding import Mesh, PartitionSpec as P

HEAD_DIM = 128
GROUPS = 8
SUB = 128
F32 = jnp.float32
BF16 = jnp.bfloat16
VMEM = pl.BlockSpec(memory_space=pltpu.VMEM)
SMEM = pl.BlockSpec(memory_space=pltpu.SMEM)
PARAMS = pltpu.CompilerParams(vmem_limit_bytes=40 * 2**20)


def softmax_rows(q, ka, va, kb, vb):
    factor = math.log2(math.e) / math.sqrt(HEAD_DIM)
    nt = (((1,), (1,)), ((), ()))
    sa = lax.dot_general(q, ka, nt, preferred_element_type=F32)
    sb = lax.dot_general(q, kb, nt, preferred_element_type=F32)
    peak = jnp.maximum(jnp.max(sa, axis=1, keepdims=True), jnp.max(sb, axis=1, keepdims=True))
    ea = jnp.exp2((sa - peak) * factor)
    eb = jnp.exp2((sb - peak) * factor)
    total = jnp.sum(ea, axis=1, keepdims=True) + jnp.sum(eb, axis=1, keepdims=True)
    acc = jnp.dot(ea.astype(BF16), va, preferred_element_type=F32)
    acc = acc + jnp.dot(eb.astype(BF16), vb, preferred_element_type=F32)
    return acc, peak * factor, total


def pack_body(rows, gw, chip_ref, keys_ref, values_ref, queries_ref, *out_refs):
    for k, out_ref in enumerate(out_refs):
        col = pl.ds(pl.multiple_of((chip_ref[0] ^ k) * gw, HEAD_DIM), gw)
        out_ref[:rows] = keys_ref[:, col]
        out_ref[rows : 2 * rows] = values_ref[:, col]
        out_ref[2 * rows :] = queries_ref[:, col]


def unpack_body(gw, chip_ref, *refs):
    out_ref = refs[-1]
    for k, piece_ref in enumerate(refs[:-1]):
        out_ref[:, pl.ds(pl.multiple_of((chip_ref[0] ^ k) * gw, HEAD_DIM), gw)] = piece_ref[...]


def attend_body(chips, rows, *refs):
    own, other, outs = refs[:chips], refs[chips : 2 * chips], refs[2 * chips :]
    heads = own[0].shape[1] // HEAD_DIM
    rows_q = own[0].shape[0] - 2 * rows
    for h in range(heads):
        col = slice(h * HEAD_DIM, (h + 1) * HEAD_DIM)

        def gather(pieces, at):
            return jnp.concatenate([r[at : at + rows, col] for r in pieces], axis=0)

        ka, va, kb, vb = gather(own, 0), gather(own, rows), gather(other, 0), gather(other, rows)
        step = SUB // rows_q
        for first in range(0, chips, step):
            q = jnp.concatenate([r[2 * rows :, col] for r in own[first : first + step]], axis=0)
            acc, _, total = softmax_rows(q, ka, va, kb, vb)
            acc = (acc / total).astype(BF16)
            for n in range(step):
                outs[first + n][:, col] = acc[n * rows_q : (n + 1) * rows_q]


def local_permutes(keys, values, queries):
    chips = lax.axis_size("chip")
    rows, width = keys.shape
    gw = width // chips
    layers, tok_rows, _ = queries.shape
    rows_q = layers * tok_rows
    chip = lax.axis_index("chip").reshape(1).astype(jnp.int32)

    def across(piece, k):
        return lax.ppermute(piece, "chip", [(i, i ^ k) for i in range(chips)]) if k else piece

    packed = pl.pallas_call(
        functools.partial(pack_body, rows, gw),
        in_specs=[SMEM, VMEM, VMEM, VMEM],
        out_specs=[VMEM] * chips,
        out_shape=[jax.ShapeDtypeStruct((2 * rows + rows_q, gw), BF16)] * chips,
        compiler_params=PARAMS,
    )(chip, keys, values, queries.reshape(rows_q, width))
    order = sorted(range(chips), key=lambda k: -k)
    own = {k: across(packed[k], k) for k in order}
    other = {k: lax.ppermute(own[k][: 2 * rows], "core", [(0, 1), (1, 0)]) for k in reversed(order)}
    outs = pl.pallas_call(
        functools.partial(attend_body, chips, rows),
        in_specs=[VMEM] * (2 * chips),
        out_specs=[VMEM] * chips,
        out_shape=[jax.ShapeDtypeStruct((rows_q, gw), BF16)] * chips,
        compiler_params=PARAMS,
    )(*[own[k] for k in range(chips)], *[other[k] for k in range(chips)])
    back = {k: across(outs[k], k) for k in order}
    result = pl.pallas_call(
        functools.partial(unpack_body, gw),
        in_specs=[SMEM] + [VMEM] * chips,
        out_specs=VMEM,
        out_shape=jax.ShapeDtypeStruct((rows_q, width), BF16),
        compiler_params=PARAMS,
    )(chip, *[back[k] for k in range(chips)])
    return result.reshape(layers, tok_rows, width)


def partial_head(q_ref, ka_ref, va_ref, kb_ref, vb_ref, o_ref, peak_ref, total_ref):
    src, rows, _ = q_ref.shape
    q = q_ref[...].reshape(src * rows, HEAD_DIM)
    kv = [r[...].reshape(-1, HEAD_DIM) for r in (ka_ref, va_ref, kb_ref, vb_ref)]
    outs = []
    for at in range(0, src * rows, SUB):
        acc, peak, total = softmax_rows(q[at : at + SUB], *kv)
        outs.append(acc)
        peak_ref[at : at + SUB] = jnp.broadcast_to(peak, (SUB, HEAD_DIM))
        total_ref[at : at + SUB] = jnp.broadcast_to(total, (SUB, HEAD_DIM))
    o_ref[...] = jnp.concatenate(outs, axis=0).reshape(o_ref.shape)


def partial_attend(got, other, rows_kv, rows_q):
    chips, _, width = got.shape
    heads = width // HEAD_DIM
    own_kv = got[:, : 2 * rows_kv].reshape(chips, 2, rows_kv, width)
    own_q = got[:, 2 * rows_kv :]
    other = other.reshape(chips, 2, rows_kv, width)

    def kv(which):
        return pl.BlockSpec((chips, None, rows_kv, HEAD_DIM), lambda h: (0, which, 0, h))

    q_spec = pl.BlockSpec((chips, rows_q, HEAD_DIM), lambda h: (0, 0, h))
    stat_spec = pl.BlockSpec((None, chips * rows_q, HEAD_DIM), lambda h: (h, 0, 0))
    stat = jax.ShapeDtypeStruct((heads, chips * rows_q, HEAD_DIM), F32)
    return pl.pallas_call(
        partial_head,
        grid=(heads,),
        in_specs=[q_spec, kv(0), kv(1), kv(0), kv(1)],
        out_specs=[q_spec, stat_spec, stat_spec],
        out_shape=[jax.ShapeDtypeStruct((chips, rows_q, width), F32), stat, stat],
        compiler_params=PARAMS,
    )(own_q, own_kv, own_kv, other, other)


def local_blocks(keys, values, queries):
    chips = lax.axis_size("chip")
    blocks = chips // GROUPS
    ctx_rows, width = keys.shape
    gw = width // GROUPS
    heads = gw // HEAD_DIM
    layers, tok_rows, _ = queries.shape
    rows_q = layers * tok_rows
    rows_kv = ctx_rows // blocks

    def by_chip(array):
        return jnp.swapaxes(array.reshape(rows_kv, chips, gw), 0, 1)

    q = jnp.swapaxes(queries.reshape(rows_q, GROUPS, gw), 0, 1)
    q = jnp.broadcast_to(q[None], (blocks, GROUPS, rows_q, gw)).reshape(chips, rows_q, gw)
    packed = jnp.concatenate([by_chip(keys), by_chip(values), q], axis=1)
    got = lax.all_to_all(packed, "chip", split_axis=0, concat_axis=0, tiled=True)
    other = lax.ppermute(got[:, : 2 * rows_kv], "core", [(0, 1), (1, 0)])
    outs = partial_attend(got, other, rows_kv, rows_q)
    stats = [jnp.moveaxis(s[:, :, 0].reshape(heads, chips, rows_q), 0, 2) for s in outs[1:]]
    stats = jnp.concatenate(stats, axis=2)
    stats = jnp.pad(stats, ((0, 0), (0, 0), (0, -2 * heads % HEAD_DIM)))
    sent = jnp.concatenate([outs[0], stats], axis=2)
    back = lax.all_to_all(sent, "chip", split_axis=0, concat_axis=0, tiled=True)
    back = back.reshape(blocks, GROUPS, rows_q, -1)
    summed = back[..., :gw].reshape(blocks, GROUPS, rows_q, heads, HEAD_DIM)
    peak = back[..., gw : gw + heads]
    total = back[..., gw + heads : gw + 2 * heads]
    share = jnp.exp2(peak - jnp.max(peak, axis=0))
    denom = jnp.sum(share * total, axis=0)
    numer = jnp.sum(share[..., None] * summed, axis=0)
    result = (numer / denom[..., None]).astype(BF16)
    return jnp.swapaxes(result.reshape(GROUPS, rows_q, gw), 0, 1).reshape(layers, tok_rows, width)


def solution(mesh):
    rep, seq = mesh.shape["rep"], mesh.shape["seq"]
    chips = seq // 2
    by_core = Mesh(mesh.devices.reshape(rep, chips, 2), ("rep", "chip", "core"))
    rows = ("rep", "chip", "core")
    return jax.shard_map(
        local_permutes if chips == GROUPS else local_blocks,
        mesh=by_core,
        in_specs=(P(rows, None), P(rows, None), P(None, rows, None)),
        out_specs=P(None, rows, None),
        check_vma=False,
    )
```

time: 89.1 us -> 83.7 us (0.939)
  blocking collectives: 73.9 us -> 0 us
  starting transfers between devices: 0.07 us -> 34.7 us
  waiting for transfers between devices: 2.95 us -> 36.6 us
    all_to_all x2 -> x0, blocking collectives: 73.9 us -> none  [the longest x1 52.9 us: local(): lax.all_to_all(packed, 'chip', split_axis=0, concat_axis=0, tiled=True)]
    ppermute x1 -> x22, starting transfers between devices: 0.07 us -> 34.7 us  [the longest x14 32.5 us: across(): lax.ppermute(piece, 'chip', [(i, i ^ k) for i in range(chips)])]
    ppermute x1 -> x22, waiting for transfers between devices: 2.95 us -> 36.6 us  [the longest x14 35.5 us: across(): lax.ppermute(piece, 'chip', [(i, i ^ k) for i in range(chips)])]
    unnamed x5 -> x6, local copies, waits for them, and re-layouts: 1.38 us -> 3.26 us
    reshape x2 -> x0, local copies, waits for them, and re-layouts: 1.21 us -> none  [the longest x1 1.14 us: local(): return jnp.swapaxes(back, 0, 1).reshape(layers, tok_rows, width)]
    pallas_call x1 -> x3, Pallas kernels: 8.41 us -> 8.17 us  [the longest x1 7.13 us: local_permutes(): pl.pallas_call(functools.partial(attend_body, chips, rows), in_specs=[VME...]
  transfers between devices with their start and end apart: 1 -> 22, of which waited for: 1 -> 9; matrix products, arithmetic and copies ran while one was open for 0% -> 0% of each run, Pallas kernels for 0% -> 0%
where the time goes in v2:
time: 83.7 us; the launch traced here: 83 us
  waiting for transfers between devices  36.6 us (44%)
  starting transfers between devices  34.7 us (41%)
  Pallas kernels  8.17 us (10%)
  local copies, waits for them, and re-layouts  3.38 us (4%)
    ppermute x14, waiting for transfers between devices, across(): lax.ppermute(piece, 'chip', [(i, i ^ k) for i in range(chips)])  35.5 us
    ppermute x14, starting transfers between devices, across(): lax.ppermute(piece, 'chip', [(i, i ^ k) for i in range(chips)])  32.5 us
    pallas_call x1, Pallas kernels, local_permutes(): pl.pallas_call(functools.partial(attend_body, chips, rows), in_specs=[VME...  7.13 us
    unnamed x6, local copies, waits for them, and re-layouts  3.26 us
    ppermute x8, starting transfers between devices, local_permutes(): lax.ppermute(own[k][:2 * rows], 'core', [(0, 1), (1, 0)])  2.24 us
  transfers between devices with their start and end apart: 22, of which 9 were waited for; matrix products, arithmetic and copies ran while one was open for 0% of the time, Pallas kernels for 0%

profile of v2, /device:TPU:0, one launch (start us, length us, event | category | flops | bytes accessed | tf_op | source)
XLA Modules:
  0.0 83.0 jit_solution(3332008251599497371)
XLA Ops:
  0.0 1.1 %copy-done = bf16[64,5120]{1,0:T(8,128)(2,1)S(1)} copy-done((bf16[64,5120]{1,0:T(8,128)(2,1)S(1)}, bf16[64,5120]{1,0:T(8,128)(2,1)}, u32[]{:S(2)}) %copy-start) | copy-done | bytes 655384
  1.1 1.1 %copy-done.1 = bf16[64,5120]{1,0:T(8,128)(2,1)S(1)} copy-done((bf16[64,5120]{1,0:T(8,128)(2,1)S(1)}, bf16[64,5120]{1,0:T(8,128)(2,1)}, u32[]{:S(2)}) %copy-start.1) | copy-done | bytes 655384
  2.2 1.1 %copy-done.2 = bf16[2,32,5120]{2,1,0:T(8,128)(2,1)S(1)} copy-done((bf16[2,32,5120]{2,1,0:T(8,128)(2,1)S(1)}, bf16[2,32,5120]{2,1,0:T(8,128)(2,1)}, u32[]{:S(2)}) %copy-start.2) | copy-done | bytes 655384
  3.4 3.0 %collective-permute-start = (bf16[192,640]{1,0:T(8,128)(2,1)S(1)}, bf16[192,640]{1,0:T(8,128)(2,1)S(1)}, u32[]{:S(2)}, u32[]{:S(2)}) collective-permute-start(bf16[192,640]{1,0:T(8,128)(2,1)S(1)} %get-tuple-element.22), channel_id=1, source_target_pairs={{0,2},{2,0},{4,6},{6,4},{8,10},{10,8},{12,14},{14,12},{1,3},{3,1},... | collective-permute-start | bytes 737288 | tf_op jit(solution)/shard_map/ppermute | solution.py:78
  6.5 1.6 %collective-permute-start.1 = (bf16[192,640]{1,0:T(8,128)(2,1)S(1)}, bf16[192,640]{1,0:T(8,128)(2,1)S(1)}, u32[]{:S(2)}, u32[]{:S(2)}) collective-permute-start(bf16[192,640]{1,0:T(8,128)(2,1)S(1)} %get-tuple-element.23), channel_id=1, source_target_pairs={{0,4},{2,6},{4,0},{6,2},{8,12},{10,14},{12,8},{14,10},{1,5},{3,7},... | collective-permute-start | bytes 737288 | tf_op jit(solution)/shard_map/ppermute | solution.py:78
  8.0 3.0 %collective-permute-start.3 = (bf16[192,640]{1,0:T(8,128)(2,1)S(1)}, bf16[192,640]{1,0:T(8,128)(2,1)S(1)}, u32[]{:S(2)}, u32[]{:S(2)}) collective-permute-start(bf16[192,640]{1,0:T(8,128)(2,1)S(1)} %get-tuple-element.25), channel_id=1, source_target_pairs={{0,8},{2,10},{4,12},{6,14},{8,0},{10,2},{12,4},{14,6},{1,9},{3,11}... | collective-permute-start | bytes 737288 | tf_op jit(solution)/shard_map/ppermute | solution.py:78
  11.0 1.3 %collective-permute-start.4 = (bf16[192,640]{1,0:T(8,128)(2,1)S(1)}, bf16[192,640]{1,0:T(8,128)(2,1)S(1)}, u32[]{:S(2)}, u32[]{:S(2)}) collective-permute-start(bf16[192,640]{1,0:T(8,128)(2,1)S(1)} %get-tuple-element.26), channel_id=1, source_target_pairs={{0,10},{2,8},{4,14},{6,12},{8,2},{10,0},{12,6},{14,4},{1,11},{3,9}... | collective-permute-start | bytes 737288 | tf_op jit(solution)/shard_map/ppermute | solution.py:78
  12.4 3.8 %collective-permute-start.5 = (bf16[192,640]{1,0:T(8,128)(2,1)S(1)}, bf16[192,640]{1,0:T(8,128)(2,1)S(1)}, u32[]{:S(2)}, u32[]{:S(2)}) collective-permute-start(bf16[192,640]{1,0:T(8,128)(2,1)S(1)} %get-tuple-element.27), channel_id=1, source_target_pairs={{0,12},{2,14},{4,8},{6,10},{8,4},{10,6},{12,0},{14,2},{1,13},{3,15... | collective-permute-start | bytes 737288 | tf_op jit(solution)/shard_map/ppermute | solution.py:78
  16.2 8.7 %collective-permute-done.1.refs_2_ = bf16[192,640]{1,0:T(8,128)(2,1)S(1)} collective-permute-done((bf16[192,640]{1,0:T(8,128)(2,1)S(1)}, bf16[192,640]{1,0:T(8,128)(2,1)S(1)}, u32[]{:S(2)}, u32[]{:S(2)}) %collective-permute-start.1) | collective-permute-done | bytes 245792 | tf_op jit(solution)/shard_map/ppermute | solution.py:78
  24.9 1.0 %collective-permute-start.6 = (bf16[192,640]{1,0:T(8,128)(2,1)S(1)}, bf16[192,640]{1,0:T(8,128)(2,1)S(1)}, u32[]{:S(2)}, u32[]{:S(2)}) collective-permute-start(bf16[192,640]{1,0:T(8,128)(2,1)S(1)} %get-tuple-element.28), channel_id=1, source_target_pairs={{0,14},{2,12},{4,10},{6,8},{8,6},{10,4},{12,2},{14,0},{1,15},{3,13... | collective-permute-start | bytes 737288 | tf_op jit(solution)/shard_map/ppermute | solution.py:78
  26.0 1.9 %collective-permute-done.2.refs_3_ = bf16[192,640]{1,0:T(8,128)(2,1)S(1)} collective-permute-done((bf16[192,640]{1,0:T(8,128)(2,1)S(1)}, bf16[192,640]{1,0:T(8,128)(2,1)S(1)}, u32[]{:S(2)}, u32[]{:S(2)}) %collective-permute-start.2) | collective-permute-done | bytes 245792 | tf_op jit(solution)/shard_map/ppermute | solution.py:78
  27.9 0.5 collective-permute-start.8
  28.4 17.1 %collective-permute-done.4.refs_5_ = bf16[192,640]{1,0:T(8,128)(2,1)S(1)} collective-permute-done((bf16[192,640]{1,0:T(8,128)(2,1)S(1)}, bf16[192,640]{1,0:T(8,128)(2,1)S(1)}, u32[]{:S(2)}, u32[]{:S(2)}) %collective-permute-start.4) | collective-permute-done | bytes 245792 | tf_op jit(solution)/shard_map/ppermute | solution.py:78
  45.6 0.6 collective-permute-start.10
  46.3 0.6 collective-permute-start.12
  46.9 0.4 collective-permute-start.14
  48.5 7.1 %shard_map.38 = (bf16[64,640]{1,0:T(8,128)(2,1)S(1)}, bf16[64,640]{1,0:T(8,128)(2,1)S(1)}, bf16[64,640]{1,0:T(8,128)(2,1)S(1)}, bf16[64,640]{1,0:T(8,128)(2,1)S(...) custom-call(bf16[192,640]{1,0:T(8,128)(2,1)S(1)} %get-tuple-element., ...), custom_call_target="tpu_custom_call" | custom-call | tf_op jit(solution)/shard_map/pallas_call | solution.py:90
  55.9 9.0 %collective-permute-start.16 = (bf16[64,640]{1,0:T(8,128)(2,1)S(1)}, bf16[64,640]{1,0:T(8,128)(2,1)S(1)}, u32[]{:S(2)}, u32[]{:S(2)}) collective-permute-start(bf16[64,640]{1,0:T(8,128)(2,1)S(1)} %get-tuple-element.31), channel_id=1, source_target_pairs={{0,4},{2,6},{4,0},{6,2},{8,12},{10,14},{12,8},{14,10},{1,5},{3,7},... | collective-permute-start | bytes 245768 | tf_op jit(solution)/shard_map/ppermute | solution.py:78
  64.8 0.7 collective-permute-start.17
  65.5 4.2 %collective-permute-start.18 = (bf16[64,640]{1,0:T(8,128)(2,1)S(1)}, bf16[64,640]{1,0:T(8,128)(2,1)S(1)}, u32[]{:S(2)}, u32[]{:S(2)}) collective-permute-start(bf16[64,640]{1,0:T(8,128)(2,1)S(1)} %get-tuple-element.33), channel_id=1, source_target_pairs={{0,8},{2,10},{4,12},{6,14},{8,0},{10,2},{12,4},{14,6},{1,9},{3,11}... | collective-permute-start | bytes 245768 | tf_op jit(solution)/shard_map/ppermute | solution.py:78
  69.7 2.4 %collective-permute-start.20 = (bf16[64,640]{1,0:T(8,128)(2,1)S(1)}, bf16[64,640]{1,0:T(8,128)(2,1)S(1)}, u32[]{:S(2)}, u32[]{:S(2)}) collective-permute-start(bf16[64,640]{1,0:T(8,128)(2,1)S(1)} %get-tuple-element.35), channel_id=1, source_target_pairs={{0,12},{2,14},{4,8},{6,10},{8,4},{10,6},{12,0},{14,2},{1,13},{3,15... | collective-permute-start | bytes 245768 | tf_op jit(solution)/shard_map/ppermute | solution.py:78
  72.1 2.4 %collective-permute-start.21 = (bf16[64,640]{1,0:T(8,128)(2,1)S(1)}, bf16[64,640]{1,0:T(8,128)(2,1)S(1)}, u32[]{:S(2)}, u32[]{:S(2)}) collective-permute-start(bf16[64,640]{1,0:T(8,128)(2,1)S(1)} %get-tuple-element.36), channel_id=1, source_target_pairs={{0,14},{2,12},{4,10},{6,8},{8,6},{10,4},{12,2},{14,0},{1,15},{3,13... | collective-permute-start | bytes 245768 | tf_op jit(solution)/shard_map/ppermute | solution.py:78
  74.4 7.7 %collective-permute-done.19.refs_5_ = bf16[64,640]{1,0:T(8,128)(2,1)S(1)} collective-permute-done((bf16[64,640]{1,0:T(8,128)(2,1)S(1)}, bf16[64,640]{1,0:T(8,128)(2,1)S(1)}, u32[]{:S(2)}, u32[]{:S(2)}) %collective-permute-start.19) | collective-permute-done | bytes 81952 | tf_op jit(solution)/shard_map/ppermute | solution.py:78
  82.1 0.9 %shard_map.39 = bf16[64,5120]{1,0:T(8,128)(2,1)} custom-call(s32[1]{0:T(128)} %bitcast.chip_ref, bf16[64,640]{1,0:T(8,128)(2,1)S(1)} %get-tuple-element.29.refs_0_, bf16[64,640]{1,0:T(8,128)(2,1)S(1)} %collective-permute-done.15.refs_1_, bf16[64,640]{1,0:T(8,128)(2,1)S(1)} %collective-permute-done.16.refs_2_, ...), custom_call_target="tpu_custom_call" | custom-call | tf_op jit(solution)/shard_map/pallas_call | solution.py:98
  (37 shorter events, 2.0 us)
Async XLA Ops:
  0.0 1.1 %copy-start = (bf16[64,5120]{1,0:T(8,128)(2,1)S(1)}, bf16[64,5120]{1,0:T(8,128)(2,1)}, u32[]{:S(2)}) copy-start(bf16[64,5120]{1,0:T(8,128)(2,1)} %keys_ref.1) | copy-start | bytes 1966084
  1.1 1.1 %copy-start.1 = (bf16[64,5120]{1,0:T(8,128)(2,1)S(1)}, bf16[64,5120]{1,0:T(8,128)(2,1)}, u32[]{:S(2)}) copy-start(bf16[64,5120]{1,0:T(8,128)(2,1)} %values_ref.1) | copy-start | bytes 1966084
  3.4 9.0 %collective-permute-start = (bf16[192,640]{1,0:T(8,128)(2,1)S(1)}, bf16[192,640]{1,0:T(8,128)(2,1)S(1)}, u32[]{:S(2)}, u32[]{:S(2)}) collective-permute-start(bf16[192,640]{1,0:T(8,128)(2,1)S(1)} %get-tuple-element.22), channel_id=1, source_target_pairs={{0,2},{2,0},{4,6},{6,4},{8,10},{10,8},{12,14},{14,12},{1,3},{3,1},... | collective-permute-start | bytes 737288 | tf_op jit(solution)/shard_map/ppermute | solution.py:78
  6.5 18.5 %collective-permute-start.1 = (bf16[192,640]{1,0:T(8,128)(2,1)S(1)}, bf16[192,640]{1,0:T(8,128)(2,1)S(1)}, u32[]{:S(2)}, u32[]{:S(2)}) collective-permute-start(bf16[192,640]{1,0:T(8,128)(2,1)S(1)} %get-tuple-element.23), channel_id=1, source_target_pairs={{0,4},{2,6},{4,0},{6,2},{8,12},{10,14},{12,8},{14,10},{1,5},{3,7},... | collective-permute-start | bytes 737288 | tf_op jit(solution)/shard_map/ppermute | solution.py:78
  8.0 19.8 %collective-permute-start.2 = (bf16[192,640]{1,0:T(8,128)(2,1)S(1)}, bf16[192,640]{1,0:T(8,128)(2,1)S(1)}, u32[]{:S(2)}, u32[]{:S(2)}) collective-permute-start(bf16[192,640]{1,0:T(8,128)(2,1)S(1)} %get-tuple-element.24), channel_id=1, source_target_pairs={{0,6},{2,4},{4,2},{6,0},{8,14},{10,12},{12,10},{14,8},{1,7},{3,5},... | collective-permute-start | bytes 737288 | tf_op jit(solution)/shard_map/ppermute | solution.py:78
  8.0 19.8 %collective-permute-start.3 = (bf16[192,640]{1,0:T(8,128)(2,1)S(1)}, bf16[192,640]{1,0:T(8,128)(2,1)S(1)}, u32[]{:S(2)}, u32[]{:S(2)}) collective-permute-start(bf16[192,640]{1,0:T(8,128)(2,1)S(1)} %get-tuple-element.25), channel_id=1, source_target_pairs={{0,8},{2,10},{4,12},{6,14},{8,0},{10,2},{12,4},{14,6},{1,9},{3,11}... | collective-permute-start | bytes 737288 | tf_op jit(solution)/shard_map/ppermute | solution.py:78
  11.0 34.5 %collective-permute-start.4 = (bf16[192,640]{1,0:T(8,128)(2,1)S(1)}, bf16[192,640]{1,0:T(8,128)(2,1)S(1)}, u32[]{:S(2)}, u32[]{:S(2)}) collective-permute-start(bf16[192,640]{1,0:T(8,128)(2,1)S(1)} %get-tuple-element.26), channel_id=1, source_target_pairs={{0,10},{2,8},{4,14},{6,12},{8,2},{10,0},{12,6},{14,4},{1,11},{3,9}... | collective-permute-start | bytes 737288 | tf_op jit(solution)/shard_map/ppermute | solution.py:78
  12.4 33.2 %collective-permute-start.5 = (bf16[192,640]{1,0:T(8,128)(2,1)S(1)}, bf16[192,640]{1,0:T(8,128)(2,1)S(1)}, u32[]{:S(2)}, u32[]{:S(2)}) collective-permute-start(bf16[192,640]{1,0:T(8,128)(2,1)S(1)} %get-tuple-element.27), channel_id=1, source_target_pairs={{0,12},{2,14},{4,8},{6,10},{8,4},{10,6},{12,0},{14,2},{1,13},{3,15... | collective-permute-start | bytes 737288 | tf_op jit(solution)/shard_map/ppermute | solution.py:78
  24.9 21.3 %collective-permute-start.6 = (bf16[192,640]{1,0:T(8,128)(2,1)S(1)}, bf16[192,640]{1,0:T(8,128)(2,1)S(1)}, u32[]{:S(2)}, u32[]{:S(2)}) collective-permute-start(bf16[192,640]{1,0:T(8,128)(2,1)S(1)} %get-tuple-element.28), channel_id=1, source_target_pairs={{0,14},{2,12},{4,10},{6,8},{8,6},{10,4},{12,2},{14,0},{1,15},{3,13... | collective-permute-start | bytes 737288 | tf_op jit(solution)/shard_map/ppermute | solution.py:78
  27.8 18.4 %collective-permute-start.7 = (bf16[128,640]{1,0:T(8,128)(2,1)S(1)}, bf16[128,640]{1,0:T(8,128)(2,1)S(1)}, u32[]{:S(2)}, u32[]{:S(2)}) collective-permute-start(bf16[128,640]{1,0:T(8,128)(2,1)S(1)} %slice.24), channel_id=1, source_target_pairs={{0,1},{1,0},{2,3},{3,2},{4,5},{5,4},{6,7},{7,6},{8,9},{9,8},{10,11... | collective-permute-start | bytes 491528 | tf_op jit(solution)/shard_map/ppermute | solution.py:89
  27.9 19.0 %collective-permute-start.8 = (bf16[128,640]{1,0:T(8,128)(2,1)S(1)}, bf16[128,640]{1,0:T(8,128)(2,1)S(1)}, u32[]{:S(2)}, u32[]{:S(2)}) collective-permute-start(bf16[128,640]{1,0:T(8,128)(2,1)S(1)} %slice.32), channel_id=1, source_target_pairs={{0,1},{1,0},{2,3},{3,2},{4,5},{5,4},{6,7},{7,6},{8,9},{9,8},{10,11... | collective-permute-start | bytes 491528 | tf_op jit(solution)/shard_map/ppermute | solution.py:89
  45.5 1.4 %collective-permute-start.9 = (bf16[128,640]{1,0:T(8,128)(2,1)S(1)}, bf16[128,640]{1,0:T(8,128)(2,1)S(1)}, u32[]{:S(2)}, u32[]{:S(2)}) collective-permute-start(bf16[128,640]{1,0:T(8,128)(2,1)S(1)} %slice.33), channel_id=1, source_target_pairs={{0,1},{1,0},{2,3},{3,2},{4,5},{5,4},{6,7},{7,6},{8,9},{9,8},{10,11... | collective-permute-start | bytes 491528 | tf_op jit(solution)/shard_map/ppermute | solution.py:89
  45.6 1.8 %collective-permute-start.10 = (bf16[128,640]{1,0:T(8,128)(2,1)S(1)}, bf16[128,640]{1,0:T(8,128)(2,1)S(1)}, u32[]{:S(2)}, u32[]{:S(2)}) collective-permute-start(bf16[128,640]{1,0:T(8,128)(2,1)S(1)} %slice.34), channel_id=1, source_target_pairs={{0,1},{1,0},{2,3},{3,2},{4,5},{5,4},{6,7},{7,6},{8,9},{9,8},{10,11... | collective-permute-start | bytes 491528 | tf_op jit(solution)/shard_map/ppermute | solution.py:89
  46.2 1.5 %collective-permute-start.11 = (bf16[128,640]{1,0:T(8,128)(2,1)S(1)}, bf16[128,640]{1,0:T(8,128)(2,1)S(1)}, u32[]{:S(2)}, u32[]{:S(2)}) collective-permute-start(bf16[128,640]{1,0:T(8,128)(2,1)S(1)} %slice.35), channel_id=1, source_target_pairs={{0,1},{1,0},{2,3},{3,2},{4,5},{5,4},{6,7},{7,6},{8,9},{9,8},{10,11... | collective-permute-start | bytes 491528 | tf_op jit(solution)/shard_map/ppermute | solution.py:89
  46.3 1.6 %collective-permute-start.12 = (bf16[128,640]{1,0:T(8,128)(2,1)S(1)}, bf16[128,640]{1,0:T(8,128)(2,1)S(1)}, u32[]{:S(2)}, u32[]{:S(2)}) collective-permute-start(bf16[128,640]{1,0:T(8,128)(2,1)S(1)} %slice.36), channel_id=1, source_target_pairs={{0,1},{1,0},{2,3},{3,2},{4,5},{5,4},{6,7},{7,6},{8,9},{9,8},{10,11... | collective-permute-start | bytes 491528 | tf_op jit(solution)/shard_map/ppermute | solution.py:89
  46.9 1.4 %collective-permute-start.13 = (bf16[128,640]{1,0:T(8,128)(2,1)S(1)}, bf16[128,640]{1,0:T(8,128)(2,1)S(1)}, u32[]{:S(2)}, u32[]{:S(2)}) collective-permute-start(bf16[128,640]{1,0:T(8,128)(2,1)S(1)} %slice.37), channel_id=1, source_target_pairs={{0,1},{1,0},{2,3},{3,2},{4,5},{5,4},{6,7},{7,6},{8,9},{9,8},{10,11... | collective-permute-start | bytes 491528 | tf_op jit(solution)/shard_map/ppermute | solution.py:89
  46.9 1.5 %collective-permute-start.14 = (bf16[128,640]{1,0:T(8,128)(2,1)S(1)}, bf16[128,640]{1,0:T(8,128)(2,1)S(1)}, u32[]{:S(2)}, u32[]{:S(2)}) collective-permute-start(bf16[128,640]{1,0:T(8,128)(2,1)S(1)} %slice.38), channel_id=1, source_target_pairs={{0,1},{1,0},{2,3},{3,2},{4,5},{5,4},{6,7},{7,6},{8,9},{9,8},{10,11... | collective-permute-start | bytes 491528 | tf_op jit(solution)/shard_map/ppermute | solution.py:89
  55.6 14.1 %collective-permute-start.15 = (bf16[64,640]{1,0:T(8,128)(2,1)S(1)}, bf16[64,640]{1,0:T(8,128)(2,1)S(1)}, u32[]{:S(2)}, u32[]{:S(2)}) collective-permute-start(bf16[64,640]{1,0:T(8,128)(2,1)S(1)} %get-tuple-element.30), channel_id=1, source_target_pairs={{0,2},{2,0},{4,6},{6,4},{8,10},{10,8},{12,14},{14,12},{1,3},{3,1},... | collective-permute-start | bytes 245768 | tf_op jit(solution)/shard_map/ppermute | solution.py:78
  55.9 16.2 %collective-permute-start.16 = (bf16[64,640]{1,0:T(8,128)(2,1)S(1)}, bf16[64,640]{1,0:T(8,128)(2,1)S(1)}, u32[]{:S(2)}, u32[]{:S(2)}) collective-permute-start(bf16[64,640]{1,0:T(8,128)(2,1)S(1)} %get-tuple-element.31), channel_id=1, source_target_pairs={{0,4},{2,6},{4,0},{6,2},{8,12},{10,14},{12,8},{14,10},{1,5},{3,7},... | collective-permute-start | bytes 245768 | tf_op jit(solution)/shard_map/ppermute | solution.py:78
  64.8 9.6 %collective-permute-start.17 = (bf16[64,640]{1,0:T(8,128)(2,1)S(1)}, bf16[64,640]{1,0:T(8,128)(2,1)S(1)}, u32[]{:S(2)}, u32[]{:S(2)}) collective-permute-start(bf16[64,640]{1,0:T(8,128)(2,1)S(1)} %get-tuple-element.32), channel_id=1, source_target_pairs={{0,6},{2,4},{4,2},{6,0},{8,14},{10,12},{12,10},{14,8},{1,7},{3,5},... | collective-permute-start | bytes 245768 | tf_op jit(solution)/shard_map/ppermute | solution.py:78
  65.5 8.9 %collective-permute-start.18 = (bf16[64,640]{1,0:T(8,128)(2,1)S(1)}, bf16[64,640]{1,0:T(8,128)(2,1)S(1)}, u32[]{:S(2)}, u32[]{:S(2)}) collective-permute-start(bf16[64,640]{1,0:T(8,128)(2,1)S(1)} %get-tuple-element.33), channel_id=1, source_target_pairs={{0,8},{2,10},{4,12},{6,14},{8,0},{10,2},{12,4},{14,6},{1,9},{3,11}... | collective-permute-start | bytes 245768 | tf_op jit(solution)/shard_map/ppermute | solution.py:78
  69.7 12.4 %collective-permute-start.19 = (bf16[64,640]{1,0:T(8,128)(2,1)S(1)}, bf16[64,640]{1,0:T(8,128)(2,1)S(1)}, u32[]{:S(2)}, u32[]{:S(2)}) collective-permute-start(bf16[64,640]{1,0:T(8,128)(2,1)S(1)} %get-tuple-element.34), channel_id=1, source_target_pairs={{0,10},{2,8},{4,14},{6,12},{8,2},{10,0},{12,6},{14,4},{1,11},{3,9}... | collective-permute-start | bytes 245768 | tf_op jit(solution)/shard_map/ppermute | solution.py:78
  69.7 12.4 %collective-permute-start.20 = (bf16[64,640]{1,0:T(8,128)(2,1)S(1)}, bf16[64,640]{1,0:T(8,128)(2,1)S(1)}, u32[]{:S(2)}, u32[]{:S(2)}) collective-permute-start(bf16[64,640]{1,0:T(8,128)(2,1)S(1)} %get-tuple-element.35), channel_id=1, source_target_pairs={{0,12},{2,14},{4,8},{6,10},{8,4},{10,6},{12,0},{14,2},{1,13},{3,15... | collective-permute-start | bytes 245768 | tf_op jit(solution)/shard_map/ppermute | solution.py:78
  72.1 10.1 %collective-permute-start.21 = (bf16[64,640]{1,0:T(8,128)(2,1)S(1)}, bf16[64,640]{1,0:T(8,128)(2,1)S(1)}, u32[]{:S(2)}, u32[]{:S(2)}) collective-permute-start(bf16[64,640]{1,0:T(8,128)(2,1)S(1)} %get-tuple-element.36), channel_id=1, source_target_pairs={{0,14},{2,12},{4,10},{6,8},{8,6},{10,4},{12,2},{14,0},{1,15},{3,13... | collective-permute-start | bytes 245768 | tf_op jit(solution)/shard_map/ppermute | solution.py:78
  (1 other events, 1.1 us)
